TPU v7x, 32 devices: a whole 2x2x4 slice. The times are simulated.
32 devices in a mesh: groups: 2 (over x), slot: 16 (over z, y, core).
Axes of the slice: x: 2, y: 2, z: 4, core: 2. Of those that a mesh axis runs over, the one named last changes fastest.
Arguments:
- timesteps: int32 [32], P(('groups', 'slot')), parts along dimension 0, may hold values from 50 to 799
- prompt_ids: int32 [154], P('groups'), parts along dimension 0, may hold values from 0 to 49407
- start_latent: float32 [8, 4, 2, 128], P('groups'), parts along dimension 0, may hold values from -6 to 6
- iterate: float32 [32, 4, 4, 2, 128], P(('groups', 'slot')), parts along dimension 0, may hold values from -6 to 6
- fresh_noise: float32 [32, 4, 4, 2, 128], P(('groups', 'slot')), parts along dimension 0, may hold values from -6 to 6
- token_table: bfloat16 [49408, 1024], P('slot'), may hold values from -6 to 6
- empty_text: float32 [1024], replicated, may hold values from -6 to 6
- time_in: bfloat16 [320, 1280], replicated, may hold values from -0.3125 to 0.3125
- time_out: bfloat16 [1280, 320], replicated, may hold values from -0.15625 to 0.15625
- text_proj: bfloat16 [1024, 320], replicated, may hold values from -0.1875 to 0.1875
- conv_first: bfloat16 [9, 320, 4], replicated, may hold values from -1 to 1
- spatial_weights: bfloat16 [2, 9, 320, 320], replicated, may hold values from -0.109375 to 0.109375
- temporal_weights: bfloat16 [2, 3, 320, 320], replicated, may hold values from -0.1875 to 0.1875
- conv_last: bfloat16 [9, 4, 320], replicated, may hold values from -0.109375 to 0.109375
Outputs:
- new_iterate: float32 [32, 4, 4, 2, 128], P(('groups', 'slot')), parts along dimension 0
- final_latent: float32 [8, 4, 2, 128], P('groups'), parts along dimension 0
There are 2 independent parts, one for each index of `groups`. A program takes and returns all parts, laid end to end along the dimension named above; an argument that names none is the same for every part. Nothing has to cross between parts.
All inputs are finite; a program needn't handle non-finite values.
Results may differ from a plain program's by a relative error of at most 0.012.
Values sent between devices are 32-bit elements; how exact they have to be, the bound alone decides.
A program may use at most 64 MiB of HBM per device.

v0:
```python
import functools

import jax
import jax.numpy as jnp
import numpy as np
from jax import lax
from jax.experimental import pallas as pl
from jax.experimental.pallas import tpu as pltpu
from jax.sharding import PartitionSpec as P

GROUPS = 32
DT = 50
NORM_EPS = 1e-05
GUIDANCE_SCALE = 5.0
LANES = 128
PAD = 1024
F32 = jnp.float32
BF16 = jnp.bfloat16


def alpha_bar(step_value):
    phase_angle = (step_value / 1000.0 + 0.008) / 1.008 * (jnp.pi / 2.0)
    cosine = jnp.cos(phase_angle)
    return cosine * cosine


def layer_norm(values):
    average = jnp.mean(values, axis=-1, keepdims=True)
    spread = jnp.mean((values - average) ** 2, axis=-1, keepdims=True)
    return (values - average) * lax.rsqrt(spread + NORM_EPS)


def silu(values):
    half = 0.5 * values
    return half + half * jnp.tanh(half)


def dot(a, b):
    return jnp.dot(a, b, preferred_element_type=F32)


def shift(tile, step):
    if step == 0:
        return tile
    lane = lax.broadcasted_iota(jnp.int32, tile.shape, 1)
    rolled = pltpu.roll(tile, (-step) % LANES, axis=1)
    return jnp.where(lane == (LANES - 1 if step == 1 else 0), 0.0, rolled)


def group_matrix(channels):
    size = channels // GROUPS
    group = lax.broadcasted_iota(jnp.int32, (GROUPS, channels), 0) * size
    channel = lax.broadcasted_iota(jnp.int32, (GROUPS, channels), 1)
    return jnp.where((channel >= group) & (channel < group + size), 1.0, 0.0).astype(BF16)


def expand_matrix(channels):
    size = channels // GROUPS
    channel = lax.broadcasted_iota(jnp.int32, (channels, 3 * GROUPS), 0)
    group = (lax.broadcasted_iota(jnp.int32, (channels, 3 * GROUPS), 1) & (GROUPS - 1)) * size
    return jnp.where((channel >= group) & (channel < group + size), 1.0, 0.0).astype(BF16)


def spread_groups(expand, stat):
    high = stat.astype(BF16)
    rest = stat - high.astype(F32)
    middle = rest.astype(BF16)
    low = (rest - middle.astype(F32)).astype(BF16)
    return dot(expand, jnp.concatenate([high, middle, low], axis=0))


def lane_means(sums, frames, count, temporal):
    if temporal:
        folded = sum(sums[:, f * LANES : (f + 1) * LANES] for f in range(frames))
        total = jnp.sum(folded, axis=1, keepdims=True) * (1.0 / (count * frames))
        return jnp.broadcast_to(total, sums.shape)
    parts = []
    for f in range(frames):
        total = jnp.sum(sums[:, f * LANES : (f + 1) * LANES], axis=1, keepdims=True)
        parts.append(jnp.broadcast_to(total * (1.0 / count), (sums.shape[0], LANES)))
    return jnp.concatenate(parts, axis=1)


def norm_silu(state, gather, expand, frames, temporal):
    rows, channels, _ = state.shape
    count = (channels // GROUPS) * rows * LANES
    sums = sum(dot(gather, state[r]) for r in range(rows))
    mean = spread_groups(expand, lane_means(sums, frames, count, temporal))
    centred = [state[r].astype(F32) - mean for r in range(rows)]
    square = sum(c * c for c in centred)
    high = square.astype(BF16)
    low = (square - high.astype(F32)).astype(BF16)
    spread = lane_means(dot(gather, high) + dot(gather, low), frames, count, temporal)
    scale = spread_groups(expand, lax.rsqrt(spread + NORM_EPS))
    return [silu(c * scale) for c in centred]


def sample_body(step_value, emb, latent, w_first, spatial, temporal, w_last, scratch, ready):
    state, xs, xt, wcat, wt, first_in = scratch
    sections, _, channels, _ = spatial.shape
    lat, frames, rows = latent.shape[1:4]
    gather = group_matrix(channels)
    expand = expand_matrix(channels)
    three = 3 * channels

    xs[...] = jnp.zeros_like(xs)
    xt[...] = jnp.zeros_like(xt)

    first_in[...] = jnp.zeros_like(first_in)
    for r in range(rows):
        for f in range(frames):
            tile = jnp.concatenate([latent[0, l, f, pl.ds(r, 1), :] for l in range(lat)], axis=0)
            for k in range(3):
                first_in[pl.ds((r + 1) * 3 * lat + k * lat, lat), pl.ds(f * LANES, LANES)] = shift(
                    tile, k - 1
                )
    ready("first")
    weight = jnp.concatenate([w_first[k].astype(F32) for k in range(9)], axis=1).astype(BF16)
    column = jnp.broadcast_to(emb, (LANES, channels)).T
    column = jnp.concatenate([column] * frames, axis=1)
    for r in range(rows):
        window = first_in[pl.ds((r * 3) * lat, 9 * lat), :] if r else first_in[pl.ds(0, 9 * lat), :]
        state[r] = (dot(weight, window.astype(BF16)) + column).astype(BF16)

    blank = jnp.zeros((channels, PAD - three), BF16)
    for s in range(sections):
        ready("spatial", s)
        for g in range(3):
            wcat[:, pl.ds(g * PAD, PAD)] = jnp.concatenate(
                [spatial[s, 3 * g + k] for k in range(3)] + [blank], axis=1
            )
        normed = norm_silu(state[...], gather, expand, frames, False)
        for r in range(rows):
            for f in range(frames):
                at = pl.ds(f * LANES, LANES)
                tile = normed[r][:, f * LANES : (f + 1) * LANES]
                for k in range(3):
                    xs[pl.ds(r * PAD + k * channels, channels), at] = shift(tile, k - 1).astype(BF16)
        for r in range(rows):
            moved = dot(wcat[:, pl.ds((1 - r) * PAD, 2 * PAD)], xs[...])
            state[r] = (state[r].astype(F32) + moved).astype(BF16)
        ready("temporal", s)
        wt[...] = jnp.concatenate([temporal[s, k] for k in range(3)] + [blank], axis=1)
        normed = norm_silu(state[...], gather, expand, frames, True)
        for r in range(rows):
            for f in range(frames):
                tile = normed[r][:, f * LANES : (f + 1) * LANES].astype(BF16)
                for k in range(3):
                    to = f - (k - 1)
                    if 0 <= to < frames:
                        xt[pl.ds(k * channels, channels), pl.ds((r * frames + to) * LANES, LANES)] = tile
        for r in range(rows):
            moved = dot(wt[...], xt[:, pl.ds(r * frames * LANES, frames * LANES)])
            state[r] = (state[r].astype(F32) + moved).astype(BF16)

    normed = norm_silu(state[...], gather, expand, frames, False)
    ready("last")
    taps = [dot(w_last[...], normed[r].astype(BF16)) for r in range(rows)]
    predicted = []
    for r in range(rows):
        per_frame = []
        for f in range(frames):
            total = None
            for k in range(3):
                tile = sum(
                    taps[q][((q - r + 1) * 3 + k) * lat :][:lat, f * LANES : (f + 1) * LANES]
                    for q in range(rows)
                )
                term = shift(tile, k - 1)
                total = term if total is None else total + term
            per_frame.append(total)
        predicted.append(per_frame)
    return predicted


def step_of(timesteps):
    return jnp.full((8, LANES), timesteps[0], jnp.int32).astype(F32)


def text_row(row, text_proj):
    pair = layer_norm(row).astype(BF16)
    return dot(jnp.broadcast_to(pair, (16, row.shape[1])), text_proj[...])[0:1]


def loader(sem, names):
    copies = {}
    for index, (key, source, target) in enumerate(names):
        copies[key] = pltpu.make_async_copy(source, target, sem.at[index])
    for copy in copies.values():
        copy.start()

    def ready(*key):
        copies[key].wait()

    return ready


def weight_copies(first_hbm, spatial_hbm, temporal_hbm, last_hbm, first, spatial, temporal, last):
    names = [(("first",), first_hbm, first)]
    for s in range(spatial_hbm.shape[0]):
        names.append((("spatial", s), spatial_hbm.at[s], spatial.at[s]))
        names.append((("temporal", s), temporal_hbm.at[s], temporal.at[s]))
    names.append((("last",), last_hbm, last))
    return names


def uncond_kernel(
    timesteps, empty, latent, time_in_hbm, time_out_hbm, text_hbm, first_hbm, spatial_hbm,
    temporal_hbm, last_hbm, pred_out, tvec_out,
    time_in, time_out, text_proj, first, spatial, temporal, last, sem, *scratch
):
    names = [
        (("time_in",), time_in_hbm, time_in),
        (("time_out",), time_out_hbm, time_out),
        (("text",), text_hbm, text_proj),
    ]
    names += weight_copies(
        first_hbm, spatial_hbm, temporal_hbm, last_hbm, first, spatial, temporal, last
    )
    ready = loader(sem, names)
    channels = time_in.shape[0]
    half = channels // 2
    lane = lax.broadcasted_iota(jnp.int32, (16, channels), 1)
    place = jnp.where(lane < half, lane, lane - half).astype(F32)
    step = jnp.full((16, channels), timesteps[0], jnp.int32).astype(F32)
    angles = step * jnp.exp(np.float32(-np.log(10000.0)) * place / half)
    feature = jnp.where(lane < half, jnp.cos(angles), jnp.sin(angles)).astype(BF16)
    ready("time_in")
    hidden = silu(dot(feature, time_in[...])).astype(BF16)
    ready("time_out")
    tvec = dot(hidden, time_out[...])[0:1]
    tvec_out[...] = tvec
    ready("text")
    emb = tvec + text_row(empty[...], text_proj)
    predicted = sample_body(None, emb, latent, first, spatial, temporal, last, scratch, ready)
    for r, per_frame in enumerate(predicted):
        for f, tile in enumerate(per_frame):
            pred_out[r, f] = tile


def cond_kernel(
    prompt, timesteps, pooled, tvec, latent, fresh, uncond, text_hbm, first_hbm, spatial_hbm,
    temporal_hbm, last_hbm, drift_out,
    text_proj, first, spatial, temporal, last, sem, *scratch
):
    names = [(("text",), text_hbm, text_proj)]
    names += weight_copies(
        first_hbm, spatial_hbm, temporal_hbm, last_hbm, first, spatial, temporal, last
    )
    ready = loader(sem, names)
    ready("text")
    emb = tvec[...] + text_row(pooled[...] * (1.0 / prompt), text_proj)
    predicted = sample_body(None, emb, latent, first, spatial, temporal, last, scratch, ready)
    step_value = step_of(timesteps)
    now = alpha_bar(step_value)
    prev = alpha_bar(step_value - DT)
    ratio = jnp.sqrt(prev / now)
    noise_square = (1.0 - prev) * (1.0 - now / prev) / (1.0 - now)
    kept_square = (1.0 - prev) * (now / prev - now) / (1.0 - now)
    eps_factor = (jnp.sqrt(kept_square) - ratio * jnp.sqrt(1.0 - now))[0:1]
    noise_factor = jnp.sqrt(noise_square)[0:1]
    keep = (ratio - 1.0)[0:1]
    lat = latent.shape[1]
    for r, per_frame in enumerate(predicted):
        for f, tile in enumerate(per_frame):
            without = uncond[r, f]
            guided = without + GUIDANCE_SCALE * (tile - without)
            for l in range(lat):
                drift_out[l, f, pl.ds(r, 1), :] = (
                    keep * latent[0, l, f, pl.ds(r, 1), :]
                    + eps_factor * guided[l : l + 1]
                    + noise_factor * fresh[0, l, f, pl.ds(r, 1), :]
                )


def exchange_kernel(
    n, drift, start, new_out, final_out, inbox, result, outbox, send1, recv1, send2, recv2, lsem
):
    pieces = drift.shape[0]
    stride = n // pieces
    me = lax.axis_index("slot")
    mine = me // stride
    owner = lax.rem(me, stride) == 0
    barrier = pltpu.get_barrier_semaphore()

    def to(slot):
        return {"slot": slot}

    for k in range(1, n):
        pl.semaphore_signal(
            barrier, inc=1, device_id=to(lax.rem(me + k, n)), device_id_type=pl.DeviceIdType.MESH
        )
    pl.semaphore_wait(barrier, n - 1)

    def first_copy(k):
        piece = lax.rem(mine + k, pieces)
        return pltpu.make_async_remote_copy(
            src_ref=drift.at[piece], dst_ref=inbox.at[me], send_sem=send1.at[k],
            recv_sem=recv1.at[me], device_id=to(piece * stride),
            device_id_type=pl.DeviceIdType.MESH,
        )

    def second_copy(k):
        slot = lax.rem(me + k, n)
        return pltpu.make_async_remote_copy(
            src_ref=result.at[slot], dst_ref=outbox.at[mine], send_sem=send2.at[k],
            recv_sem=recv2.at[mine], device_id=to(slot), device_id_type=pl.DeviceIdType.MESH,
        )

    for k in range(1, pieces):
        first_copy(k).start()

    if stride > 1:
        @pl.when(jnp.logical_not(owner))
        def _():
            first_copy(0).start()

    @pl.when(owner)
    def _():
        inbox[me] = drift[mine]
        for k in range(1, n):
            slot = lax.rem(me + k, n)
            pltpu.make_async_remote_copy(
                src_ref=drift.at[mine], dst_ref=inbox.at[slot], send_sem=send1.at[0],
                recv_sem=recv1.at[slot], device_id=to(slot), device_id_type=pl.DeviceIdType.MESH,
            ).wait_recv()
        running = start[mine]
        for j in range(n):
            result[j, 0] = running
            running = running + inbox[j]
        for j in range(n):
            result[j, 1] = running
        for k in range(1, n):
            second_copy(k).start()
        outbox[mine] = result[me]

    for k in range(1, pieces):
        piece = lax.rem(mine + k, pieces)
        pltpu.make_async_remote_copy(
            src_ref=result.at[0], dst_ref=outbox.at[piece], send_sem=send2.at[0],
            recv_sem=recv2.at[piece], device_id=to(piece * stride),
            device_id_type=pl.DeviceIdType.MESH,
        ).wait_recv()
    if stride > 1:
        @pl.when(jnp.logical_not(owner))
        def _():
            pltpu.make_async_remote_copy(
                src_ref=result.at[0], dst_ref=outbox.at[mine], send_sem=send2.at[0],
                recv_sem=recv2.at[mine], device_id=to(mine * stride),
                device_id_type=pl.DeviceIdType.MESH,
            ).wait_recv()
            first_copy(0).wait_send()
    new_out[...] = outbox[:, 0]
    final_out[...] = outbox[:, 1]
    for k in range(1, pieces):
        first_copy(k).wait_send()

    @pl.when(owner)
    def _():
        for k in range(1, n):
            second_copy(k).wait_send()


VMEM = pl.BlockSpec(memory_space=pltpu.VMEM)
SMEM = pl.BlockSpec(memory_space=pltpu.SMEM)
ANY = pl.BlockSpec(memory_space=pl.ANY)


def like(array):
    return pltpu.VMEM(array.shape, array.dtype)


def local(
    timesteps, prompt_ids, start_latent, iterate, fresh_noise, token_table, empty_text, time_in,
    time_out, text_proj, conv_first, spatial_weights, temporal_weights, conv_last,
):
    n = lax.axis_size("slot")
    shard_rows = token_table.shape[0]
    local_ids = prompt_ids - lax.axis_index("slot") * shard_rows
    counts = jnp.sum(
        (local_ids[:, None] == jnp.arange(shard_rows, dtype=jnp.int32)[None, :]).astype(F32),
        axis=0, keepdims=True,
    ).astype(BF16)
    partial_sum = jnp.dot(counts, token_table, preferred_element_type=F32)
    pooled = lax.psum(partial_sum, "slot")

    lat, frames, rows, cols = iterate.shape[1:]
    sections, _, channels, _ = spatial_weights.shape
    last = conv_last.reshape(9 * lat, channels)
    width = frames * cols
    scratch = [
        pltpu.VMEM((rows, channels, width), BF16),
        pltpu.VMEM((rows * PAD, width), BF16),
        pltpu.VMEM((PAD, rows * width), BF16),
        pltpu.VMEM((channels, 3 * PAD), BF16),
        pltpu.VMEM((channels, PAD), BF16),
        pltpu.VMEM((12 * lat, width), F32),
    ]
    weights = [conv_first, spatial_weights, temporal_weights, last]
    count = 2 + 2 * sections
    cost = pl.CostEstimate(flops=4_000_000_000, bytes_accessed=7_000_000, transcendentals=1_600_000)
    params = pltpu.CompilerParams(vmem_limit_bytes=48 * 1024 * 1024)
    uncond, tvec = pl.pallas_call(
        uncond_kernel,
        out_shape=(
            jax.ShapeDtypeStruct((rows, frames, lat, cols), F32),
            jax.ShapeDtypeStruct((1, channels), F32),
        ),
        in_specs=[SMEM, VMEM, VMEM] + [ANY] * 7,
        out_specs=(VMEM, VMEM),
        scratch_shapes=[like(time_in), like(time_out), like(text_proj)]
        + [like(w) for w in weights]
        + [pltpu.SemaphoreType.DMA((3 + count,))]
        + scratch,
        compiler_params=params,
        cost_estimate=cost,
        name="uncond_sample",
    )(timesteps, empty_text[None], iterate, time_in, time_out, text_proj, *weights)
    drift = pl.pallas_call(
        functools.partial(cond_kernel, prompt_ids.shape[0]),
        out_shape=jax.ShapeDtypeStruct((lat, frames, rows, cols), F32),
        in_specs=[SMEM] + [VMEM] * 5 + [ANY] * 5,
        out_specs=VMEM,
        scratch_shapes=[like(text_proj)]
        + [like(w) for w in weights]
        + [pltpu.SemaphoreType.DMA((1 + count,))]
        + scratch,
        compiler_params=params,
        cost_estimate=cost,
        name="cond_sample",
    )(timesteps, pooled, tvec, iterate, fresh_noise, uncond, text_proj, *weights)

    pieces = lat * frames
    piece = (rows, cols)
    shape = jax.ShapeDtypeStruct((pieces,) + piece, F32)
    new, final = pl.pallas_call(
        functools.partial(exchange_kernel, n),
        out_shape=(shape, shape),
        in_specs=[VMEM, VMEM],
        out_specs=(VMEM, VMEM),
        scratch_shapes=[
            pltpu.VMEM((n,) + piece, F32),
            pltpu.VMEM((n, 2) + piece, F32),
            pltpu.VMEM((pieces, 2) + piece, F32),
            pltpu.SemaphoreType.DMA((pieces,)),
            pltpu.SemaphoreType.DMA((n,)),
            pltpu.SemaphoreType.DMA((n,)),
            pltpu.SemaphoreType.DMA((pieces,)),
            pltpu.SemaphoreType.DMA,
        ],
        compiler_params=pltpu.CompilerParams(collective_id=0, has_side_effects=True),
        name="exchange",
    )(drift.reshape(shape.shape), start_latent.reshape(shape.shape))
    return new.reshape(iterate.shape), final.reshape(start_latent.shape)


def solution(mesh):
    placed = (
        P(("groups", "slot")),
        P("groups"),
        P("groups", None, None, None),
        P(("groups", "slot"), None, None, None, None),
        P(("groups", "slot"), None, None, None, None),
        P("slot", None),
    ) + (P(),) * 8
    return jax.shard_map(
        local,
        mesh=mesh,
        in_specs=placed,
        out_specs=(P(("groups", "slot"), None, None, None, None), P("groups", None, None, None)),
        check_vma=False,
    )
```

profile of v0, /device:TPU:0, one launch (start us, length us, event | category | flops | bytes accessed | tf_op | source)
XLA Modules:
  0.0 94.2 jit_solution(7417169587237811179)
XLA Ops:
  0.6 1.4 %copy.22.text_hbm = bf16[1024,320]{1,0:T(8,128)(2,1)S(1)} copy(bf16[1024,320]{0,1:T(8,128)(2,1)} %param.23) | data formatting | bytes 1310720 | tf_op args[9]
  2.1 1.2 %copy.23.first_hbm = bf16[9,320,4]{2,1,0:T(8,128)(2,1)S(1)} copy(bf16[9,320,4]{1,2,0:T(4,128)(2,1)} %param.24) | data formatting | bytes 46080 | tf_op args[10]
  3.3 0.8 reshape.24.last_hbm
  4.7 1.5 %copy.21.time_out_hbm = bf16[1280,320]{1,0:T(8,128)(2,1)S(1)} copy(bf16[1280,320]{0,1:T(8,128)(2,1)} %param.22) | data formatting | bytes 1638400 | tf_op args[8]
  6.2 0.0 copy-start.1
  6.3 1.4 %copy-done.1 = bf16[2,3,320,320]{3,2,1,0:T(8,128)(2,1)S(1)} copy-done((bf16[2,3,320,320]{3,2,1,0:T(8,128)(2,1)S(1)}, bf16[2,3,320,320]{3,2,1,0:T(8,128)(2,1)}, u32[]{:S(2)}) %copy-start.1) | copy-done | bytes 1228824
  7.6 1.1 %copy-done.3 = bf16[320,1280]{1,0:T(8,128)(2,1)S(1)} copy-done((bf16[320,1280]{1,0:T(8,128)(2,1)S(1)}, bf16[320,1280]{1,0:T(8,128)(2,1)}, u32[]{:S(2)}) %copy-start.3) | copy-done | bytes 819224
  8.8 0.7 copy-done.4
  9.5 0.7 copy-done.7
  10.2 15.2 %uncond_sample.1 = (f32[2,4,4,128]{3,2,1,0:T(4,128)S(1)}, f32[1,320]{1,0:T(1,128)S(1)}) custom-call(s32[1]{0:T(128)S(6)} %copy.28.timesteps, f32[1,1024]{1,0:T(1,128)S(1)} %bitcast.9, f32[1,4,4,2,128]{4,3,2,1,0:T(2,128)S(1)} %copy-done.4, bf16[320,1280]{1,0:T(8,128)(2,1)S(1)} %copy-done.3, bf16[1280,320]{1,0:T(8,128)(2,1)S(1)} %copy.21.time_out_hbm, ...), custom_call_target="tpu_custom_call" | custom-call | flops 4000000000 | bytes 7000000 | tf_op jit(solution)/shard_map/uncond_sample/pallas_call | solution.py:403
  25.3 0.0 copy-start.5
  25.4 0.0 copy-start.6
  25.4 0.0 copy-done.8
  25.4 0.2 convert_reduce_fusion
  25.6 3.7 %fusion = f32[1,1024]{1,0:T(1,128)S(1)} fusion(bf16[3088,1]{0,1:T(2,128)(2,1)S(1)} %reshape.29, bf16[3088,1024]{1,0:T(8,128)(2,1)} %param.19), kind=kOutput, calls=%fused_computation.3 | convolution fusion | flops 6324224 | bytes 6334496 | tf_op jit(solution)/shard_map/dot_general | solution.py:384
  29.3 35.1 %psum.7.pooled = f32[1,1024]{1,0:T(1,128)S(1)} all-reduce(f32[1,1024]{1,0:T(1,128)S(1)} %fusion), channel_id=1, replica_groups=mesh['groups'=2,'slot'=16] {'slot'}, use_global_device_ids=true, to_apply=%region_1.0 | all-reduce | flops 1024 | bytes 8192 | tf_op jit(solution)/shard_map/psum | solution.py:385
  64.5 0.0 copy-start.2
  64.5 1.4 %copy-done.2 = bf16[2,3,320,320]{3,2,1,0:T(8,128)(2,1)S(1)} copy-done((bf16[2,3,320,320]{3,2,1,0:T(8,128)(2,1)S(1)}, bf16[2,3,320,320]{3,2,1,0:T(8,128)(2,1)}, u32[]{:S(2)}) %copy-start.2) | copy-done | bytes 1228824
  65.8 14.3 %cond_sample.1 = f32[4,4,2,128]{3,2,1,0:T(2,128)S(1)} custom-call(s32[1]{0:T(128)S(6)} %copy.28.timesteps, f32[1,1024]{1,0:T(1,128)S(1)} %psum.7.pooled, f32[1,320]{1,0:T(1,128)S(1)} %get-tuple-element.6.tvec, f32[1,4,4,2,128]{4,3,2,1,0:T(2,128)S(1)} %copy-done.5, f32[1,4,4,2,128]{4,3,2,1,0:T(2,128)S(1)} %copy-done.6, ...), custom_call_target="tpu_custom_call" | custom-call | flops 4000000000 | bytes 7000000 | tf_op jit(solution)/shard_map/cond_sample/pallas_call | solution.py:419
  80.2 0.0 copy-start
  80.2 0.6 copy-done
  80.8 10.7 %exchange.1 = (f32[16,2,128]{2,1,0:T(2,128)}, f32[16,2,128]{2,1,0:T(2,128)}) custom-call(f32[16,2,128]{2,1,0:T(2,128)} %bitcast.8, f32[16,2,128]{2,1,0:T(2,128)} %bitcast.10), custom_call_target="tpu_custom_call" | custom-call | tf_op jit(solution)/shard_map/exchange/pallas_call | solution.py:436
  91.5 1.3 %copy.29 = f32[1,4,4,2,128]{4,3,2,1,0:T(2,128)} copy(f32[1,4,4,2,128]{4,3,2,1,0:T(2,128)} %bitcast.12) | data formatting | bytes 32768
  92.9 1.3 %copy.30 = f32[4,4,2,128]{3,2,1,0:T(2,128)} copy(f32[4,4,2,128]{3,2,1,0:T(2,128)} %bitcast.11) | data formatting | bytes 32768
  (8 shorter events, 0.0 us)
Async XLA Ops:
  6.2 1.4 %copy-start.1 = (bf16[2,3,320,320]{3,2,1,0:T(8,128)(2,1)S(1)}, bf16[2,3,320,320]{3,2,1,0:T(8,128)(2,1)}, u32[]{:S(2)}) copy-start(bf16[2,3,320,320]{3,2,1,0:T(8,128)(2,1)} %temporal_hbm.3) | copy-start | bytes 3686404
  7.6 1.1 %copy-start.3 = (bf16[320,1280]{1,0:T(8,128)(2,1)S(1)}, bf16[320,1280]{1,0:T(8,128)(2,1)}, u32[]{:S(2)}) copy-start(bf16[320,1280]{1,0:T(8,128)(2,1)} %time_in_hbm.1) | copy-start | bytes 2457604
  8.8 0.7 copy-start.4
  9.5 0.7 copy-start.7
  10.2 15.2 %copy-start.8 = (s32[77]{0:T(128)S(1)}, s32[77]{0:T(128)}, u32[]{:S(2)}) copy-start(s32[77]{0:T(128)} %param.15) | copy-start | bytes 928
  25.3 39.1 %copy-start.5 = (f32[1,4,4,2,128]{4,3,2,1,0:T(2,128)S(1)}, f32[1,4,4,2,128]{4,3,2,1,0:T(2,128)}, u32[]{:S(2)}) copy-start(f32[1,4,4,2,128]{4,3,2,1,0:T(2,128)} %latent.3) | copy-start | bytes 49156
  25.4 39.1 %copy-start.6 = (f32[1,4,4,2,128]{4,3,2,1,0:T(2,128)S(1)}, f32[1,4,4,2,128]{4,3,2,1,0:T(2,128)}, u32[]{:S(2)}) copy-start(f32[1,4,4,2,128]{4,3,2,1,0:T(2,128)} %fresh.1) | copy-start | bytes 49156
  64.5 1.4 %copy-start.2 = (bf16[2,3,320,320]{3,2,1,0:T(8,128)(2,1)S(1)}, bf16[2,3,320,320]{3,2,1,0:T(8,128)(2,1)}, u32[]{:S(2)}) copy-start(bf16[2,3,320,320]{3,2,1,0:T(8,128)(2,1)} %temporal_hbm.3) | copy-start | bytes 3686404
  80.2 0.6 copy-start
where the time goes:
time: 94.9 us; the launch traced here: 94.2 us
  Pallas kernels  40.2 us (42%)
  blocking collectives  35.1 us (37%)
  local copies, waits for them, and re-layouts  13.5 us (14%)
  matrix products  3.72 us (4%)
  between operations  1.42 us (1%)
    psum x1, blocking collectives, local(): pooled = lax.psum(partial_sum, 'slot')  35.1 us
    pallas_call x1, Pallas kernels, local(): pl.pallas_call(uncond_kernel, out_shape=(jax.ShapeDtypeStruct((rows, fram...  15.2 us
    pallas_call x1, Pallas kernels, local(): pl.pallas_call(functools.partial(cond_kernel, prompt_ids.shape[0]), out_s...  14.3 us
    unnamed x23, local copies, waits for them, and re-layouts  12.7 us
    pallas_call x1, Pallas kernels, local(): pl.pallas_call(functools.partial(exchange_kernel, n), out_shape=(shape, s...  10.7 us
    dot_general x1, matrix products, local(): partial_sum = jnp.dot(counts, token_table, preferred_element_type=F32)  3.72 us

commit v1 on v0

v1 whole, which is shorter than its diff:
```python
import functools

import jax
import jax.numpy as jnp
import numpy as np
from jax import lax
from jax.experimental import pallas as pl
from jax.experimental.pallas import tpu as pltpu
from jax.sharding import PartitionSpec as P

GROUPS = 32
DT = 50
NORM_EPS = 1e-05
GUIDANCE_SCALE = 5.0
LANES = 128
PAD = 1024
F32 = jnp.float32
BF16 = jnp.bfloat16
LEAD = 3


def alpha_bar(step_value):
    phase_angle = (step_value / 1000.0 + 0.008) / 1.008 * (jnp.pi / 2.0)
    cosine = jnp.cos(phase_angle)
    return cosine * cosine


def layer_norm(values):
    average = jnp.mean(values, axis=-1, keepdims=True)
    spread = jnp.mean((values - average) ** 2, axis=-1, keepdims=True)
    return (values - average) * lax.rsqrt(spread + NORM_EPS)


def silu(values):
    half = 0.5 * values
    return half + half * jnp.tanh(half)


def dot(a, b):
    return jnp.dot(a, b, preferred_element_type=F32)


def shift(tile, step):
    if step == 0:
        return tile
    lane = lax.broadcasted_iota(jnp.int32, tile.shape, 1)
    rolled = pltpu.roll(tile, (-step) % LANES, axis=1)
    return jnp.where(lane == (LANES - 1 if step == 1 else 0), 0.0, rolled)


def group_matrix(channels):
    size = channels // GROUPS
    group = lax.broadcasted_iota(jnp.int32, (GROUPS, channels), 0) * size
    channel = lax.broadcasted_iota(jnp.int32, (GROUPS, channels), 1)
    return jnp.where((channel >= group) & (channel < group + size), 1.0, 0.0).astype(BF16)


def expand_matrix(channels):
    size = channels // GROUPS
    channel = lax.broadcasted_iota(jnp.int32, (channels, 3 * GROUPS), 0)
    group = (lax.broadcasted_iota(jnp.int32, (channels, 3 * GROUPS), 1) & (GROUPS - 1)) * size
    return jnp.where((channel >= group) & (channel < group + size), 1.0, 0.0).astype(BF16)


def spread_groups(expand, stat):
    high = stat.astype(BF16)
    rest = stat - high.astype(F32)
    middle = rest.astype(BF16)
    low = (rest - middle.astype(F32)).astype(BF16)
    return dot(expand, jnp.concatenate([high, middle, low], axis=0))


def lane_means(sums, frames, count, temporal):
    if temporal:
        folded = sum(sums[:, f * LANES : (f + 1) * LANES] for f in range(frames))
        total = jnp.sum(folded, axis=1, keepdims=True) * (1.0 / (count * frames))
        return jnp.broadcast_to(total, sums.shape)
    parts = []
    for f in range(frames):
        total = jnp.sum(sums[:, f * LANES : (f + 1) * LANES], axis=1, keepdims=True)
        parts.append(jnp.broadcast_to(total * (1.0 / count), (sums.shape[0], LANES)))
    return jnp.concatenate(parts, axis=1)


def norm_silu(state, gather, expand, frames, temporal):
    rows, channels, _ = state.shape
    count = (channels // GROUPS) * rows * LANES
    sums = sum(dot(gather, state[r]) for r in range(rows))
    mean = spread_groups(expand, lane_means(sums, frames, count, temporal))
    centred = [state[r].astype(F32) - mean for r in range(rows)]
    square = sum(c * c for c in centred)
    high = square.astype(BF16)
    low = (square - high.astype(F32)).astype(BF16)
    spread = lane_means(dot(gather, high) + dot(gather, low), frames, count, temporal)
    scale = spread_groups(expand, lax.rsqrt(spread + NORM_EPS))
    return [silu(c * scale) for c in centred]


def dot_nt(a, b):
    return lax.dot_general(a, b, (((1,), (1,)), ((), ())), preferred_element_type=F32)


def small_taps(weight, rows):
    taps = [weight[k].astype(F32) for k in range(9)]
    lat, channels = taps[0].shape
    return jnp.concatenate(taps + [jnp.zeros((rows - 9 * lat, channels), F32)], axis=0)


def first_windows(latent, first_in):
    lat, frames, rows = latent.shape[1:4]
    first_in[...] = jnp.zeros_like(first_in)
    for r in range(rows):
        for f in range(frames):
            tile = jnp.concatenate([latent[0, l, f, pl.ds(r, 1), :] for l in range(lat)], axis=0)
            for k in range(3):
                first_in[pl.ds((r + 1) * 3 * lat + k * lat, lat), pl.ds(f * LANES, LANES)] = shift(
                    tile, k - 1
                )


def sample_steps(emb, weight, first_in, wcat, wt, w_last, scratch, consts, sizes, predicted, ready):
    state, xs, xt = scratch
    gather, expand = consts
    sections, channels, lat, frames, rows = sizes
    column = jnp.broadcast_to(emb, (LANES, channels)).T
    column = jnp.concatenate([column] * frames, axis=1)
    for r in range(rows):
        window = first_in[pl.ds(r * 3 * lat, weight.shape[1]), :].astype(BF16)
        state[r] = (dot(weight, window) + column).astype(BF16)
    yield
    for s in range(sections):
        normed = norm_silu(state[...], gather, expand, frames, False)
        for r in range(rows):
            for f in range(frames):
                at = pl.ds(f * LANES, LANES)
                tile = normed[r][:, f * LANES : (f + 1) * LANES]
                for k in range(3):
                    xs[pl.ds(r * PAD + k * channels, channels), at] = shift(tile, k - 1).astype(BF16)
        yield
        ready("spatial", s)
        for r in range(rows):
            moved = dot(wcat[s, :, pl.ds((1 - r) * PAD, 2 * PAD)], xs[...])
            state[r] = (state[r].astype(F32) + moved).astype(BF16)
        yield
        normed = norm_silu(state[...], gather, expand, frames, True)
        for r in range(rows):
            for f in range(frames):
                tile = normed[r][:, f * LANES : (f + 1) * LANES].astype(BF16)
                for k in range(3):
                    to = f - (k - 1)
                    if 0 <= to < frames:
                        xt[pl.ds(k * channels, channels), pl.ds((r * frames + to) * LANES, LANES)] = tile
        yield
        ready("temporal", s)
        for r in range(rows):
            moved = dot(wt[s], xt[:, pl.ds(r * frames * LANES, frames * LANES)])
            state[r] = (state[r].astype(F32) + moved).astype(BF16)
        yield
    normed = norm_silu(state[...], gather, expand, frames, False)
    yield
    ready("last")
    taps_last = small_taps(w_last, 48).astype(BF16)
    taps = [dot(taps_last, normed[r].astype(BF16)) for r in range(rows)]
    for r in range(rows):
        for f in range(frames):
            total = None
            for k in range(3):
                tile = sum(
                    taps[q][((q - r + 1) * 3 + k) * lat :][:lat, f * LANES : (f + 1) * LANES]
                    for q in range(rows)
                )
                term = shift(tile, k - 1)
                total = term if total is None else total + term
            predicted[r][f] = total
    yield


def text_row(row, text_proj):
    pair = layer_norm(row).astype(BF16)
    return dot_nt(jnp.broadcast_to(pair, (16, row.shape[1])), text_proj[...])[0:1]


def time_row(timesteps, time_in, time_out, ready):
    channels = time_in.shape[0]
    half = channels // 2
    lane = lax.broadcasted_iota(jnp.int32, (16, channels), 1)
    place = jnp.where(lane < half, lane, lane - half).astype(F32)
    step = jnp.full((16, channels), timesteps[0], jnp.int32).astype(F32)
    angles = step * jnp.exp(np.float32(-np.log(10000.0)) * place / half)
    feature = jnp.where(lane < half, jnp.cos(angles), jnp.sin(angles)).astype(BF16)
    ready("time_in")
    hidden = silu(dot(feature, time_in[...])).astype(BF16)
    ready("time_out")
    return dot_nt(hidden, time_out[...])[0:1]


def drift_factors(timesteps):
    step_value = jnp.full((8, LANES), timesteps[0], jnp.int32).astype(F32)
    now = alpha_bar(step_value)
    prev = alpha_bar(step_value - DT)
    ratio = jnp.sqrt(prev / now)
    noise_square = (1.0 - prev) * (1.0 - now / prev) / (1.0 - now)
    kept_square = (1.0 - prev) * (now / prev - now) / (1.0 - now)
    eps_factor = (jnp.sqrt(kept_square) - ratio * jnp.sqrt(1.0 - now))[0:1]
    return (ratio - 1.0)[0:1], eps_factor, jnp.sqrt(noise_square)[0:1]


def token_counts(prompt, shard_rows, me):
    amount = prompt.shape[0]
    base = me * shard_rows
    sub = lax.broadcasted_iota(jnp.int32, (16, LANES), 0)
    wide = -(-shard_rows // LANES) * LANES
    lane = lax.broadcasted_iota(jnp.int32, (16, wide), 1)
    counts = jnp.zeros((16, wide), F32)
    for start in range(0, amount, 16):
        column = jnp.full((16, LANES), -1, jnp.int32)
        for j in range(min(16, amount - start)):
            column = jnp.where(sub == j, prompt[start + j] - base, column)
        column = jnp.concatenate([column] * (wide // LANES), axis=1)
        counts = counts + jnp.where(lane == column, 1.0, 0.0)
    return counts[:, :shard_rows].astype(BF16)


def sweep_kernel(
    n, prompt, timesteps, empty, start, latent, fresh, first, last, table_hbm, time_in_hbm,
    time_out_hbm, text_hbm, spatial_hbm, temporal_hbm, result_out,
    table, time_in, time_out, text_proj, spatial, temporal, sem,
    wcat, wt, first_in, state_u, xs_u, xt_u, state_c, xs_c, xt_c,
    partial, pool, drift, inbox, result, outbox, sendp, recvp, send1, recv1, send2, recv2,
):
    mesh_id = pl.DeviceIdType.MESH
    sections, _, channels, _ = spatial.shape
    lat, frames, rows = latent.shape[1:4]
    me = lax.axis_index("slot")
    barrier = pltpu.get_barrier_semaphore()

    def to(slot):
        return {"slot": slot}

    copies = {}
    names = [
        (("time_in",), time_in_hbm, time_in),
        (("time_out",), time_out_hbm, time_out),
        (("text",), text_hbm, text_proj),
        (("table",), table_hbm, table),
    ]
    for s in range(sections):
        names.append((("spatial", s), spatial_hbm.at[s], spatial.at[s]))
        names.append((("temporal", s), temporal_hbm.at[s], temporal.at[s]))
    for index, (key, source, target) in enumerate(names):
        copies[key] = pltpu.make_async_copy(source, target, sem.at[index])
        copies[key].start()
    for k in range(1, n):
        pl.semaphore_signal(barrier, inc=1, device_id=to(lax.rem(me + k, n)), device_id_type=mesh_id)

    done = set()
    blank = jnp.zeros((channels, PAD - 3 * channels), BF16)

    def ready(*key):
        if key in done:
            return
        done.add(key)
        if key in copies:
            copies[key].wait()
        if key[0] == "spatial":
            s = key[1]
            for g in range(3):
                wcat[s, :, pl.ds(g * PAD, PAD)] = jnp.concatenate(
                    [spatial[s, 3 * g + k] for k in range(3)] + [blank], axis=1
                )
        if key[0] == "temporal":
            s = key[1]
            wt[s] = jnp.concatenate([temporal[s, k] for k in range(3)] + [blank], axis=1)

    for ref in (xs_u, xs_c):
        for r in range(rows):
            ref[pl.ds(r * PAD + 3 * channels, PAD - 3 * channels), :] = jnp.zeros(
                (PAD - 3 * channels, ref.shape[1]), BF16
            )
    for ref in (xt_u, xt_c):
        ref[...] = jnp.zeros_like(ref)
    counts = token_counts(prompt, table.shape[0], me)
    first_windows(latent, first_in)
    weight = small_taps(first, 40).T.astype(BF16)
    consts = (group_matrix(channels), expand_matrix(channels))
    sizes = (sections, channels, lat, frames, rows)
    keep, eps_factor, noise_factor = drift_factors(timesteps)
    tvec = time_row(timesteps, time_in, time_out, ready)
    ready("text")
    emb_u = tvec + text_row(empty[...], text_proj)

    ready("table")
    partial[...] = jnp.sum(dot(counts, table[...]), axis=0, keepdims=True)
    pl.semaphore_wait(barrier, n - 1)

    def pooled_copy(k):
        return pltpu.make_async_remote_copy(
            src_ref=partial, dst_ref=pool.at[me], send_sem=sendp.at[k], recv_sem=recvp.at[me],
            device_id=to(lax.rem(me + k, n)), device_id_type=mesh_id,
        )

    for k in range(1, n):
        pooled_copy(k).start()
    pool[me] = partial[...]

    pred_u = [[None] * frames for _ in range(rows)]
    pred_c = [[None] * frames for _ in range(rows)]
    steps_u = sample_steps(
        emb_u, weight, first_in, wcat, wt, last, (state_u, xs_u, xt_u), consts, sizes, pred_u, ready
    )
    for _ in range(LEAD):
        next(steps_u)

    for s in range(sections):
        ready("spatial", s)
        ready("temporal", s)
    for k in range(1, n):
        slot = lax.rem(me + k, n)
        pltpu.make_async_remote_copy(
            src_ref=partial, dst_ref=pool.at[slot], send_sem=sendp.at[0], recv_sem=recvp.at[slot],
            device_id=to(slot), device_id_type=mesh_id,
        ).wait_recv()
    pooled = pool[0]
    for k in range(1, n):
        pooled = pooled + pool[k]
    emb_c = tvec + text_row(pooled * (1.0 / prompt.shape[0]), text_proj)
    steps_c = sample_steps(
        emb_c, weight, first_in, wcat, wt, last, (state_c, xs_c, xt_c), consts, sizes, pred_c, ready
    )
    live = True
    while live:
        live = next(steps_c, 0) is None
        next(steps_u, 0)

    for r in range(rows):
        for f in range(frames):
            without = pred_u[r][f]
            guided = without + GUIDANCE_SCALE * (pred_c[r][f] - without)
            for l in range(lat):
                drift[l * frames + f, pl.ds(r, 1), :] = (
                    keep * latent[0, l, f, pl.ds(r, 1), :]
                    + eps_factor * guided[l : l + 1]
                    + noise_factor * fresh[0, l, f, pl.ds(r, 1), :]
                )
    exchange(
        n, me, to, drift, start, result_out, inbox, result, outbox, send1, recv1, send2, recv2
    )
    for k in range(1, n):
        pooled_copy(k).wait_send()


def exchange(
    n, me, to, drift, start, result_out, inbox, result, outbox, send1, recv1, send2, recv2
):
    pieces = drift.shape[0]
    stride = n // pieces
    mine = me // stride if stride > 1 else me
    mesh_id = pl.DeviceIdType.MESH

    def for_owner(body):
        pl.when(lax.rem(me, stride) == 0)(body) if stride > 1 else body()

    def for_others(body):
        if stride > 1:
            pl.when(lax.rem(me, stride) != 0)(body)

    def first_copy(k):
        piece = lax.rem(mine + k, pieces)
        return pltpu.make_async_remote_copy(
            src_ref=drift.at[piece], dst_ref=inbox.at[me], send_sem=send1.at[k],
            recv_sem=recv1.at[me], device_id=to(piece * stride), device_id_type=mesh_id,
        )

    def second_copy(k):
        slot = lax.rem(me + k, n)
        return pltpu.make_async_remote_copy(
            src_ref=result.at[slot], dst_ref=outbox.at[mine], send_sem=send2.at[k],
            recv_sem=recv2.at[mine], device_id=to(slot), device_id_type=mesh_id,
        )

    def second_wait(piece):
        pltpu.make_async_remote_copy(
            src_ref=result.at[0], dst_ref=outbox.at[piece], send_sem=send2.at[0],
            recv_sem=recv2.at[piece], device_id=to(piece * stride), device_id_type=mesh_id,
        ).wait_recv()

    for k in range(1, pieces):
        first_copy(k).start()
    for_others(lambda: first_copy(0).start())

    def own():
        inbox[me] = drift[mine]
        for k in range(1, n):
            slot = lax.rem(me + k, n)
            pltpu.make_async_remote_copy(
                src_ref=drift.at[mine], dst_ref=inbox.at[slot], send_sem=send1.at[0],
                recv_sem=recv1.at[slot], device_id=to(slot), device_id_type=mesh_id,
            ).wait_recv()
        running = start[mine]
        for j in range(n):
            result[j, 0] = running
            running = running + inbox[j]
        for j in range(n):
            result[j, 1] = running
        for k in range(1, n):
            second_copy(k).start()
        outbox[mine] = result[me]

    for_owner(own)
    for k in range(1, pieces):
        second_wait(lax.rem(mine + k, pieces))

    def rest():
        second_wait(mine)
        first_copy(0).wait_send()

    for_others(rest)
    result_out[...] = outbox[...]
    for k in range(1, pieces):
        first_copy(k).wait_send()

    def sent():
        for k in range(1, n):
            second_copy(k).wait_send()

    for_owner(sent)


def split_kernel(both, new_out, final_out):
    new_out[...] = both[:, 0]
    final_out[...] = both[:, 1]


VMEM = pl.BlockSpec(memory_space=pltpu.VMEM)
SMEM = pl.BlockSpec(memory_space=pltpu.SMEM)
ANY = pl.BlockSpec(memory_space=pl.ANY)


def like(array):
    return pltpu.VMEM(array.shape, array.dtype)


def local(
    timesteps, prompt_ids, start_latent, iterate, fresh_noise, token_table, empty_text, time_in,
    time_out, text_proj, conv_first, spatial_weights, temporal_weights, conv_last,
):
    n = lax.axis_size("slot")
    lat, frames, rows, cols = iterate.shape[1:]
    sections, _, channels, _ = spatial_weights.shape
    width = frames * cols
    pieces = lat * frames
    piece = (rows, cols)
    time_out, text_proj = time_out.T, text_proj.T
    conv_first = conv_first.transpose(0, 2, 1)
    sample = [
        pltpu.VMEM((rows, channels, width), BF16),
        pltpu.VMEM((rows * PAD, width), BF16),
        pltpu.VMEM((PAD, rows * width), BF16),
    ]
    big = [token_table, time_in, time_out, text_proj, spatial_weights, temporal_weights]
    both = pl.pallas_call(
        functools.partial(sweep_kernel, n),
        out_shape=jax.ShapeDtypeStruct((pieces, 2) + piece, F32),
        in_specs=[SMEM] * 2 + [VMEM] * 6 + [ANY] * 6,
        out_specs=VMEM,
        scratch_shapes=[like(w) for w in big]
        + [
            pltpu.SemaphoreType.DMA((4 + 2 * sections,)),
            pltpu.VMEM((sections, channels, 3 * PAD), BF16),
            pltpu.VMEM((sections, channels, PAD), BF16),
            pltpu.VMEM((56, width), F32),
        ]
        + sample * 2
        + [
            pltpu.VMEM((1, token_table.shape[1]), F32),
            pltpu.VMEM((n, 1, token_table.shape[1]), F32),
            pltpu.VMEM((pieces,) + piece, F32),
            pltpu.VMEM((n,) + piece, F32),
            pltpu.VMEM((n, 2) + piece, F32),
            pltpu.VMEM((pieces, 2) + piece, F32),
            pltpu.SemaphoreType.DMA((n,)),
            pltpu.SemaphoreType.DMA((n,)),
            pltpu.SemaphoreType.DMA((pieces,)),
            pltpu.SemaphoreType.DMA((n,)),
            pltpu.SemaphoreType.DMA((n,)),
            pltpu.SemaphoreType.DMA((pieces,)),
        ],
        compiler_params=pltpu.CompilerParams(
            collective_id=0, has_side_effects=True, vmem_limit_bytes=56 * 1024 * 1024
        ),
        cost_estimate=pl.CostEstimate(
            flops=8_000_000_000, bytes_accessed=14_000_000, transcendentals=3_300_000
        ),
        name="sweep",
    )(
        prompt_ids, timesteps, empty_text[None], start_latent.reshape((pieces,) + piece), iterate,
        fresh_noise, conv_first, conv_last, *big,
    )
    shape = jax.ShapeDtypeStruct((pieces,) + piece, F32)
    new, final = pl.pallas_call(
        split_kernel, out_shape=(shape, shape), in_specs=[VMEM], out_specs=(VMEM, VMEM), name="split"
    )(both)
    return new.reshape(iterate.shape), final.reshape(start_latent.shape)


def solution(mesh):
    placed = (
        P(("groups", "slot")),
        P("groups"),
        P("groups", None, None, None),
        P(("groups", "slot"), None, None, None, None),
        P(("groups", "slot"), None, None, None, None),
        P("slot", None),
    ) + (P(),) * 8
    return jax.shard_map(
        local,
        mesh=mesh,
        in_specs=placed,
        out_specs=(P(("groups", "slot"), None, None, None, None), P("groups", None, None, None)),
        check_vma=False,
    )
```

time: 94.9 us -> 44.1 us (0.46)
  blocking collectives: 35.1 us -> 0 us
  local copies, waits for them, and re-layouts: 13.5 us -> 0 us
  matrix products: 3.72 us -> 0 us
  Pallas kernels: 40.2 us -> 42.5 us
    psum x1 -> x0, blocking collectives: 35.1 us -> none  [local(): pooled = lax.psum(partial_sum, 'slot')]
    unnamed x23 -> x0, local copies, waits for them, and re-layouts: 12.7 us -> none
    dot_general x1 -> x0, matrix products: 3.72 us -> none  [local(): partial_sum = jnp.dot(counts, token_table, preferred_element_type=F32)]
    pallas_call x3 -> x2, Pallas kernels: 40.2 us -> 42.5 us  [the longest x1 41.1 us: local(): pl.pallas_call(functools.partial(sweep_kernel, n), out_shape=jax.ShapeDty...]
where the time goes in v1:
time: 44.1 us; the launch traced here: 43.8 us
  Pallas kernels  42.5 us (96%)
  between operations  1.29 us (3%)
    pallas_call x1, Pallas kernels, local(): pl.pallas_call(functools.partial(sweep_kernel, n), out_shape=jax.ShapeDty...  41.1 us
    pallas_call x1, Pallas kernels, local(): pl.pallas_call(split_kernel, out_shape=(shape, shape), in_specs=[VMEM], o...  1.38 us

profile of v1, /device:TPU:0, one launch (start us, length us, event | category | flops | bytes accessed | tf_op | source)
XLA Modules:
  0.0 43.8 jit_solution(9407907251005349839)
XLA Ops:
  1.3 41.1 %sweep.1.both = f32[16,2,2,128]{3,2,1,0:T(2,128)} custom-call(s32[77]{0:T(128)} %prompt.1, s32[1]{0:T(128)S(6)} %copy.16.timesteps, f32[1,1024]{1,0:T(1,128)} %bitcast.13, f32[16,2,128]{2,1,0:T(2,128)} %bitcast.10, f32[1,4,4,2,128]{4,3,2,1,0:T(2,128)} %latent.1, f32[1,4,4,2,128]{4,3,2,1,0:T(2,128)} %fresh.1, bf16[9,4,320]{2,1,0:T(4,128)(2,1)} %bitcast.9, ...), custom_call_target="tpu_custom_call" | custom-call | flops 8000000000 | bytes 14000000 | tf_op jit(solution)/shard_map/sweep/pallas_call | solution.py:461
  42.4 1.4 %split.1 = (f32[16,2,128]{2,1,0:T(2,128)}, f32[16,2,128]{2,1,0:T(2,128)}) custom-call(f32[16,2,2,128]{3,2,1,0:T(2,128)} %sweep.1.both), custom_call_target="tpu_custom_call" | custom-call | tf_op jit(solution)/shard_map/split/pallas_call | solution.py:500

commit v2 on v1

--- a/solution.py
+++ b/solution.py
@@ -17,6 +17,7 @@
 F32 = jnp.float32
 BF16 = jnp.bfloat16
 LEAD = 3
+EARLY = 2
 
 
 def alpha_bar(step_value):
@@ -48,11 +49,12 @@
     return jnp.where(lane == (LANES - 1 if step == 1 else 0), 0.0, rolled)
 
 
-def group_matrix(channels):
+def group_matrix(channels, copies):
     size = channels // GROUPS
     group = lax.broadcasted_iota(jnp.int32, (GROUPS, channels), 0) * size
     channel = lax.broadcasted_iota(jnp.int32, (GROUPS, channels), 1)
-    return jnp.where((channel >= group) & (channel < group + size), 1.0, 0.0).astype(BF16)
+    one = jnp.where((channel >= group) & (channel < group + size), 1.0, 0.0)
+    return jnp.concatenate([one] * copies, axis=1).astype(BF16)
 
 
 def expand_matrix(channels):
@@ -71,29 +73,47 @@
 
 
 def lane_means(sums, frames, count, temporal):
+    tiles = [sums[:, f * LANES : (f + 1) * LANES] for f in range(frames)]
     if temporal:
-        folded = sum(sums[:, f * LANES : (f + 1) * LANES] for f in range(frames))
-        total = jnp.sum(folded, axis=1, keepdims=True) * (1.0 / (count * frames))
-        return jnp.broadcast_to(total, sums.shape)
-    parts = []
-    for f in range(frames):
-        total = jnp.sum(sums[:, f * LANES : (f + 1) * LANES], axis=1, keepdims=True)
-        parts.append(jnp.broadcast_to(total * (1.0 / count), (sums.shape[0], LANES)))
-    return jnp.concatenate(parts, axis=1)
-
-
-def norm_silu(state, gather, expand, frames, temporal):
-    rows, channels, _ = state.shape
+        tiles = [sum(tiles)]
+        count = count * frames
+    means = [jnp.sum(tile, axis=1, keepdims=True) * (1.0 / count) for tile in tiles]
+    return jnp.concatenate([jnp.broadcast_to(m, (GROUPS, LANES)) for m in means], axis=1)
+
+
+def norm_silu(state, gather, expand, sizes, temporal):
+    _, channels, _, frames, rows = sizes
     count = (channels // GROUPS) * rows * LANES
-    sums = sum(dot(gather, state[r]) for r in range(rows))
-    mean = spread_groups(expand, lane_means(sums, frames, count, temporal))
-    centred = [state[r].astype(F32) - mean for r in range(rows)]
-    square = sum(c * c for c in centred)
+    values = [state[pl.ds(r * channels, channels), :].astype(F32) for r in range(rows)]
+    mean = lane_means(dot(gather, state[...]), frames, count, temporal)
+    square = sum(v * v for v in values)
     high = square.astype(BF16)
     low = (square - high.astype(F32)).astype(BF16)
-    spread = lane_means(dot(gather, high) + dot(gather, low), frames, count, temporal)
-    scale = spread_groups(expand, lax.rsqrt(spread + NORM_EPS))
-    return [silu(c * scale) for c in centred]
+    total = dot(gather, jnp.concatenate([high, low], axis=0))
+    spread = jnp.maximum(lane_means(total, frames, count, temporal) - mean * mean, 0.0)
+    scale = 0.5 * lax.rsqrt(spread + NORM_EPS)
+    both = spread_groups(expand, jnp.concatenate([scale, -mean * scale], axis=1))
+    width = scale.shape[1]
+    tiles = []
+    for r in range(rows):
+        tiles.append([])
+        for f in range(frames):
+            at = 0 if temporal else f * LANES
+            half = (
+                values[r][:, f * LANES : (f + 1) * LANES] * both[:, at : at + LANES]
+                + both[:, width + at : width + at + LANES]
+            ).astype(BF16)
+            tiles[r].append(half + half * jnp.tanh(half))
+    return tiles
+
+
+def shift_short(tile, step):
+    if step == 0:
+        return tile
+    blank = jnp.zeros((tile.shape[0], 1), tile.dtype)
+    if step == 1:
+        return jnp.concatenate([tile[:, 1:], blank], axis=1)
+    return jnp.concatenate([blank, tile[:, :-1]], axis=1)
 
 
 def dot_nt(a, b):
@@ -126,41 +146,43 @@
     column = jnp.concatenate([column] * frames, axis=1)
     for r in range(rows):
         window = first_in[pl.ds(r * 3 * lat, weight.shape[1]), :].astype(BF16)
-        state[r] = (dot(weight, window) + column).astype(BF16)
+        state[pl.ds(r * channels, channels), :] = (dot(weight, window) + column).astype(BF16)
     yield
     for s in range(sections):
-        normed = norm_silu(state[...], gather, expand, frames, False)
+        normed = norm_silu(state, gather, expand, sizes, False)
         for r in range(rows):
             for f in range(frames):
                 at = pl.ds(f * LANES, LANES)
-                tile = normed[r][:, f * LANES : (f + 1) * LANES]
                 for k in range(3):
-                    xs[pl.ds(r * PAD + k * channels, channels), at] = shift(tile, k - 1).astype(BF16)
+                    xs[pl.ds(r * PAD + k * channels, channels), at] = shift_short(
+                        normed[r][f], k - 1
+                    )
         yield
         ready("spatial", s)
         for r in range(rows):
             moved = dot(wcat[s, :, pl.ds((1 - r) * PAD, 2 * PAD)], xs[...])
-            state[r] = (state[r].astype(F32) + moved).astype(BF16)
+            at = pl.ds(r * channels, channels)
+            state[at, :] = (state[at, :].astype(F32) + moved).astype(BF16)
         yield
-        normed = norm_silu(state[...], gather, expand, frames, True)
+        normed = norm_silu(state, gather, expand, sizes, True)
         for r in range(rows):
             for f in range(frames):
-                tile = normed[r][:, f * LANES : (f + 1) * LANES].astype(BF16)
                 for k in range(3):
                     to = f - (k - 1)
                     if 0 <= to < frames:
-                        xt[pl.ds(k * channels, channels), pl.ds((r * frames + to) * LANES, LANES)] = tile
+                        xt[pl.ds(k * channels, channels), pl.ds((r * frames + to) * LANES, LANES)] = normed[r][f]
         yield
         ready("temporal", s)
         for r in range(rows):
             moved = dot(wt[s], xt[:, pl.ds(r * frames * LANES, frames * LANES)])
-            state[r] = (state[r].astype(F32) + moved).astype(BF16)
+            at = pl.ds(r * channels, channels)
+            state[at, :] = (state[at, :].astype(F32) + moved).astype(BF16)
         yield
-    normed = norm_silu(state[...], gather, expand, frames, False)
+    normed = norm_silu(state, gather, expand, sizes, False)
     yield
     ready("last")
     taps_last = small_taps(w_last, 48).astype(BF16)
-    taps = [dot(taps_last, normed[r].astype(BF16)) for r in range(rows)]
+    taps = [dot(taps_last, jnp.concatenate(normed[r], axis=1)) for r in range(rows)]
     for r in range(rows):
         for f in range(frames):
             total = None
@@ -282,13 +304,21 @@
     counts = token_counts(prompt, table.shape[0], me)
     first_windows(latent, first_in)
     weight = small_taps(first, 40).T.astype(BF16)
-    consts = (group_matrix(channels), expand_matrix(channels))
+    consts = (group_matrix(channels, rows), expand_matrix(channels))
     sizes = (sections, channels, lat, frames, rows)
     keep, eps_factor, noise_factor = drift_factors(timesteps)
     tvec = time_row(timesteps, time_in, time_out, ready)
     ready("text")
     emb_u = tvec + text_row(empty[...], text_proj)
 
+    pred_u = [[None] * frames for _ in range(rows)]
+    pred_c = [[None] * frames for _ in range(rows)]
+    steps_u = sample_steps(
+        emb_u, weight, first_in, wcat, wt, last, (state_u, xs_u, xt_u), consts, sizes, pred_u, ready
+    )
+    for _ in range(EARLY):
+        next(steps_u)
+
     ready("table")
     partial[...] = jnp.sum(dot(counts, table[...]), axis=0, keepdims=True)
     pl.semaphore_wait(barrier, n - 1)
@@ -303,12 +333,7 @@
         pooled_copy(k).start()
     pool[me] = partial[...]
 
-    pred_u = [[None] * frames for _ in range(rows)]
-    pred_c = [[None] * frames for _ in range(rows)]
-    steps_u = sample_steps(
-        emb_u, weight, first_in, wcat, wt, last, (state_u, xs_u, xt_u), consts, sizes, pred_u, ready
-    )
-    for _ in range(LEAD):
+    for _ in range(LEAD - EARLY):
         next(steps_u)
 
     for s in range(sections):
@@ -453,7 +478,7 @@
     time_out, text_proj = time_out.T, text_proj.T
     conv_first = conv_first.transpose(0, 2, 1)
     sample = [
-        pltpu.VMEM((rows, channels, width), BF16),
+        pltpu.VMEM((rows * channels, width), BF16),
         pltpu.VMEM((rows * PAD, width), BF16),
         pltpu.VMEM((PAD, rows * width), BF16),
     ]

time: 44.1 us -> 40 us (0.907)
  Pallas kernels: 42.5 us -> 38.5 us
    pallas_call x1, Pallas kernels: 41.1 us -> 37.1 us  [local(): pl.pallas_call(functools.partial(sweep_kernel, n), out_shape=jax.ShapeDty...]
where the time goes in v2:
time: 40 us; the launch traced here: 39.8 us
  Pallas kernels  38.5 us (96%)
  between operations  1.29 us (3%)
    pallas_call x1, Pallas kernels, local(): pl.pallas_call(functools.partial(sweep_kernel, n), out_shape=jax.ShapeDty...  37.1 us
    pallas_call x1, Pallas kernels, local(): pl.pallas_call(split_kernel, out_shape=(shape, shape), in_specs=[VMEM], o...  1.38 us

profile of v2, /device:TPU:0, one launch (start us, length us, event | category | flops | bytes accessed | tf_op | source)
XLA Modules:
  0.0 39.8 jit_solution(9917478505214491589)
XLA Ops:
  1.3 37.1 %sweep.1.both = f32[16,2,2,128]{3,2,1,0:T(2,128)} custom-call(s32[77]{0:T(128)} %prompt.1, s32[1]{0:T(128)S(6)} %copy.16.timesteps, f32[1,1024]{1,0:T(1,128)} %bitcast.13, f32[16,2,128]{2,1,0:T(2,128)} %bitcast.10, f32[1,4,4,2,128]{4,3,2,1,0:T(2,128)} %latent.1, f32[1,4,4,2,128]{4,3,2,1,0:T(2,128)} %fresh.1, bf16[9,4,320]{2,1,0:T(4,128)(2,1)} %bitcast.9, ...), custom_call_target="tpu_custom_call" | custom-call | flops 8000000000 | bytes 14000000 | tf_op jit(solution)/shard_map/sweep/pallas_call | solution.py:486
  38.4 1.4 %split.1 = (f32[16,2,128]{2,1,0:T(2,128)}, f32[16,2,128]{2,1,0:T(2,128)}) custom-call(f32[16,2,2,128]{3,2,1,0:T(2,128)} %sweep.1.both), custom_call_target="tpu_custom_call" | custom-call | tf_op jit(solution)/shard_map/split/pallas_call | solution.py:525

commit v3 on v2

--- a/solution.py
+++ b/solution.py
@@ -16,8 +16,8 @@
 PAD = 1024
 F32 = jnp.float32
 BF16 = jnp.bfloat16
-LEAD = 3
-EARLY = 2
+LEAD = 6
+EARLY = 4
 
 
 def alpha_bar(step_value):
@@ -72,39 +72,51 @@
     return dot(expand, jnp.concatenate([high, middle, low], axis=0))
 
 
-def lane_means(sums, frames, count, temporal):
-    tiles = [sums[:, f * LANES : (f + 1) * LANES] for f in range(frames)]
-    if temporal:
-        tiles = [sum(tiles)]
-        count = count * frames
-    means = [jnp.sum(tile, axis=1, keepdims=True) * (1.0 / count) for tile in tiles]
+def lane_means(sums, frames, count):
+    means = [
+        jnp.sum(sums[:, f * LANES : (f + 1) * LANES], axis=1, keepdims=True) * (1.0 / count)
+        for f in range(frames)
+    ]
     return jnp.concatenate([jnp.broadcast_to(m, (GROUPS, LANES)) for m in means], axis=1)
 
 
-def norm_silu(state, gather, expand, sizes, temporal):
+def split_terms(value):
+    high = value.astype(BF16)
+    low = (value - high.astype(F32)).astype(BF16)
+    return jnp.concatenate([high, low], axis=0)
+
+
+def norm_factors(state, gather, expand, sizes, temporal):
     _, channels, _, frames, rows = sizes
     count = (channels // GROUPS) * rows * LANES
     values = [state[pl.ds(r * channels, channels), :].astype(F32) for r in range(rows)]
-    mean = lane_means(dot(gather, state[...]), frames, count, temporal)
     square = sum(v * v for v in values)
-    high = square.astype(BF16)
-    low = (square - high.astype(F32)).astype(BF16)
-    total = dot(gather, jnp.concatenate([high, low], axis=0))
-    spread = jnp.maximum(lane_means(total, frames, count, temporal) - mean * mean, 0.0)
+    if temporal:
+        plain = sum(values)
+        both = [
+            split_terms(sum(v[:, f * LANES : (f + 1) * LANES] for f in range(frames)))
+            for v in (plain, square)
+        ]
+        total = dot(gather, jnp.concatenate(both, axis=1))
+        mean = lane_means(total[:, :LANES], 1, count * frames)
+        power = lane_means(total[:, LANES:], 1, count * frames)
+    else:
+        mean = lane_means(dot(gather, state[...]), frames, count)
+        power = lane_means(dot(gather, split_terms(square)), frames, count)
+    spread = jnp.maximum(power - mean * mean, 0.0)
     scale = 0.5 * lax.rsqrt(spread + NORM_EPS)
     both = spread_groups(expand, jnp.concatenate([scale, -mean * scale], axis=1))
     width = scale.shape[1]
-    tiles = []
-    for r in range(rows):
-        tiles.append([])
-        for f in range(frames):
-            at = 0 if temporal else f * LANES
-            half = (
-                values[r][:, f * LANES : (f + 1) * LANES] * both[:, at : at + LANES]
-                + both[:, width + at : width + at + LANES]
-            ).astype(BF16)
-            tiles[r].append(half + half * jnp.tanh(half))
-    return tiles
+    return both[:, :width], both[:, width:]
+
+
+def norm_tile(state, factors, sizes, r, f):
+    channels = sizes[1]
+    scale, bias = factors
+    at = f * LANES if scale.shape[1] > LANES else 0
+    value = state[pl.ds(r * channels, channels), pl.ds(f * LANES, LANES)].astype(F32)
+    half = (value * scale[:, at : at + LANES] + bias[:, at : at + LANES]).astype(BF16)
+    return half + half * jnp.tanh(half)
 
 
 def shift_short(tile, step):
@@ -148,37 +160,45 @@
         window = first_in[pl.ds(r * 3 * lat, weight.shape[1]), :].astype(BF16)
         state[pl.ds(r * channels, channels), :] = (dot(weight, window) + column).astype(BF16)
     yield
+    yield
+    half = frames // 2
+    width = half * LANES
     for s in range(sections):
-        normed = norm_silu(state, gather, expand, sizes, False)
+        factors = norm_factors(state, gather, expand, sizes, False)
+        yield
         for r in range(rows):
             for f in range(frames):
                 at = pl.ds(f * LANES, LANES)
+                tile = norm_tile(state, factors, sizes, r, f)
                 for k in range(3):
-                    xs[pl.ds(r * PAD + k * channels, channels), at] = shift_short(
-                        normed[r][f], k - 1
-                    )
+                    xs[pl.ds(r * PAD + k * channels, channels), at] = shift_short(tile, k - 1)
         yield
         ready("spatial", s)
-        for r in range(rows):
-            moved = dot(wcat[s, :, pl.ds((1 - r) * PAD, 2 * PAD)], xs[...])
-            at = pl.ds(r * channels, channels)
-            state[at, :] = (state[at, :].astype(F32) + moved).astype(BF16)
+        for part in range(2):
+            at = pl.ds(part * width, width)
+            moved = dot(wcat[s], xs[:, at])
+            state[:, at] = (state[:, at].astype(F32) + moved).astype(BF16)
+            yield
+        factors = norm_factors(state, gather, expand, sizes, True)
         yield
-        normed = norm_silu(state, gather, expand, sizes, True)
         for r in range(rows):
             for f in range(frames):
+                tile = norm_tile(state, factors, sizes, r, f)
                 for k in range(3):
                     to = f - (k - 1)
                     if 0 <= to < frames:
-                        xt[pl.ds(k * channels, channels), pl.ds((r * frames + to) * LANES, LANES)] = normed[r][f]
+                        at = pl.ds((r * frames + to) * LANES, LANES)
+                        xt[pl.ds(k * channels, channels), at] = tile
         yield
         ready("temporal", s)
         for r in range(rows):
             moved = dot(wt[s], xt[:, pl.ds(r * frames * LANES, frames * LANES)])
             at = pl.ds(r * channels, channels)
             state[at, :] = (state[at, :].astype(F32) + moved).astype(BF16)
-        yield
-    normed = norm_silu(state, gather, expand, sizes, False)
+            yield
+    factors = norm_factors(state, gather, expand, sizes, False)
+    yield
+    normed = [[norm_tile(state, factors, sizes, r, f) for f in range(frames)] for r in range(rows)]
     yield
     ready("last")
     taps_last = small_taps(w_last, 48).astype(BF16)
@@ -287,9 +307,13 @@
         if key[0] == "spatial":
             s = key[1]
             for g in range(3):
-                wcat[s, :, pl.ds(g * PAD, PAD)] = jnp.concatenate(
+                block = jnp.concatenate(
                     [spatial[s, 3 * g + k] for k in range(3)] + [blank], axis=1
                 )
+                for r in range(rows):
+                    q = r + g - 1
+                    if 0 <= q < rows:
+                        wcat[s, pl.ds(r * channels, channels), pl.ds(q * PAD, PAD)] = block
         if key[0] == "temporal":
             s = key[1]
             wt[s] = jnp.concatenate([temporal[s, k] for k in range(3)] + [blank], axis=1)
@@ -491,7 +515,7 @@
         scratch_shapes=[like(w) for w in big]
         + [
             pltpu.SemaphoreType.DMA((4 + 2 * sections,)),
-            pltpu.VMEM((sections, channels, 3 * PAD), BF16),
+            pltpu.VMEM((sections, rows * channels, rows * PAD), BF16),
             pltpu.VMEM((sections, channels, PAD), BF16),
             pltpu.VMEM((56, width), F32),
         ]

time: 40 us -> 40.3 us (level)
  no operation moved by 1% of the time
where the time goes in v3:
time: 40.3 us; the launch traced here: 40.1 us
  Pallas kernels  38.8 us (96%)
  between operations  1.29 us (3%)
    pallas_call x1, Pallas kernels, local(): pl.pallas_call(functools.partial(sweep_kernel, n), out_shape=jax.ShapeDty...  37.4 us
    pallas_call x1, Pallas kernels, local(): pl.pallas_call(split_kernel, out_shape=(shape, shape), in_specs=[VMEM], o...  1.38 us

profile of v3, /device:TPU:0, one launch (start us, length us, event | category | flops | bytes accessed | tf_op | source)
XLA Modules:
  0.0 40.1 jit_solution(6587401891405850435)
XLA Ops:
  1.3 37.4 %sweep.1.both = f32[16,2,2,128]{3,2,1,0:T(2,128)} custom-call(s32[77]{0:T(128)} %prompt.1, s32[1]{0:T(128)S(6)} %copy.16.timesteps, f32[1,1024]{1,0:T(1,128)} %bitcast.13, f32[16,2,128]{2,1,0:T(2,128)} %bitcast.10, f32[1,4,4,2,128]{4,3,2,1,0:T(2,128)} %latent.1, f32[1,4,4,2,128]{4,3,2,1,0:T(2,128)} %fresh.1, bf16[9,4,320]{2,1,0:T(4,128)(2,1)} %bitcast.9, ...), custom_call_target="tpu_custom_call" | custom-call | flops 8000000000 | bytes 14000000 | tf_op jit(solution)/shard_map/sweep/pallas_call | solution.py:510
  38.7 1.4 %split.1 = (f32[16,2,128]{2,1,0:T(2,128)}, f32[16,2,128]{2,1,0:T(2,128)}) custom-call(f32[16,2,2,128]{3,2,1,0:T(2,128)} %sweep.1.both), custom_call_target="tpu_custom_call" | custom-call | tf_op jit(solution)/shard_map/split/pallas_call | solution.py:549

commit v4 on v3

--- a/solution.py
+++ b/solution.py
@@ -16,8 +16,6 @@
 PAD = 1024
 F32 = jnp.float32
 BF16 = jnp.bfloat16
-LEAD = 6
-EARLY = 4
 
 
 def alpha_bar(step_value):
@@ -150,7 +148,7 @@
                 )
 
 
-def sample_steps(emb, weight, first_in, wcat, wt, w_last, scratch, consts, sizes, predicted, ready):
+def sample(emb, weight, first_in, wcat, wt, w_last, scratch, consts, sizes, predicted):
     state, xs, xt = scratch
     gather, expand = consts
     sections, channels, lat, frames, rows = sizes
@@ -159,28 +157,19 @@
     for r in range(rows):
         window = first_in[pl.ds(r * 3 * lat, weight.shape[1]), :].astype(BF16)
         state[pl.ds(r * channels, channels), :] = (dot(weight, window) + column).astype(BF16)
-    yield
-    yield
-    half = frames // 2
-    width = half * LANES
-    for s in range(sections):
+    width = frames * LANES
+
+    def section(s, carry):
         factors = norm_factors(state, gather, expand, sizes, False)
-        yield
         for r in range(rows):
             for f in range(frames):
                 at = pl.ds(f * LANES, LANES)
                 tile = norm_tile(state, factors, sizes, r, f)
                 for k in range(3):
                     xs[pl.ds(r * PAD + k * channels, channels), at] = shift_short(tile, k - 1)
-        yield
-        ready("spatial", s)
-        for part in range(2):
-            at = pl.ds(part * width, width)
-            moved = dot(wcat[s], xs[:, at])
-            state[:, at] = (state[:, at].astype(F32) + moved).astype(BF16)
-            yield
+        moved = dot(wcat[s], xs[...])
+        state[...] = (state[...].astype(F32) + moved).astype(BF16)
         factors = norm_factors(state, gather, expand, sizes, True)
-        yield
         for r in range(rows):
             for f in range(frames):
                 tile = norm_tile(state, factors, sizes, r, f)
@@ -189,18 +178,15 @@
                     if 0 <= to < frames:
                         at = pl.ds((r * frames + to) * LANES, LANES)
                         xt[pl.ds(k * channels, channels), at] = tile
-        yield
-        ready("temporal", s)
         for r in range(rows):
-            moved = dot(wt[s], xt[:, pl.ds(r * frames * LANES, frames * LANES)])
+            moved = dot(wt[s], xt[:, pl.ds(r * width, width)])
             at = pl.ds(r * channels, channels)
             state[at, :] = (state[at, :].astype(F32) + moved).astype(BF16)
-            yield
+        return carry
+
+    lax.fori_loop(0, sections, section, 0)
     factors = norm_factors(state, gather, expand, sizes, False)
-    yield
     normed = [[norm_tile(state, factors, sizes, r, f) for f in range(frames)] for r in range(rows)]
-    yield
-    ready("last")
     taps_last = small_taps(w_last, 48).astype(BF16)
     taps = [dot(taps_last, jnp.concatenate(normed[r], axis=1)) for r in range(rows)]
     for r in range(rows):
@@ -213,8 +199,7 @@
                 )
                 term = shift(tile, k - 1)
                 total = term if total is None else total + term
-            predicted[r][f] = total
-    yield
+            predicted[r, f] = total
 
 
 def text_row(row, text_proj):
@@ -267,7 +252,7 @@
     n, prompt, timesteps, empty, start, latent, fresh, first, last, table_hbm, time_in_hbm,
     time_out_hbm, text_hbm, spatial_hbm, temporal_hbm, result_out,
     table, time_in, time_out, text_proj, spatial, temporal, sem,
-    wcat, wt, first_in, state_u, xs_u, xt_u, state_c, xs_c, xt_c,
+    wcat, wt, first_in, state, xs, xt, emb, predicted, weight_ref,
     partial, pool, drift, inbox, result, outbox, sendp, recvp, send1, recv1, send2, recv2,
 ):
     mesh_id = pl.DeviceIdType.MESH
@@ -318,30 +303,21 @@
             s = key[1]
             wt[s] = jnp.concatenate([temporal[s, k] for k in range(3)] + [blank], axis=1)
 
-    for ref in (xs_u, xs_c):
-        for r in range(rows):
-            ref[pl.ds(r * PAD + 3 * channels, PAD - 3 * channels), :] = jnp.zeros(
-                (PAD - 3 * channels, ref.shape[1]), BF16
-            )
-    for ref in (xt_u, xt_c):
-        ref[...] = jnp.zeros_like(ref)
+    for r in range(rows):
+        xs[pl.ds(r * PAD + 3 * channels, PAD - 3 * channels), :] = jnp.zeros(
+            (PAD - 3 * channels, xs.shape[1]), BF16
+        )
+    xt[...] = jnp.zeros_like(xt)
     counts = token_counts(prompt, table.shape[0], me)
     first_windows(latent, first_in)
-    weight = small_taps(first, 40).T.astype(BF16)
+    weight_ref[...] = small_taps(first, 40).T.astype(BF16)
     consts = (group_matrix(channels, rows), expand_matrix(channels))
     sizes = (sections, channels, lat, frames, rows)
     keep, eps_factor, noise_factor = drift_factors(timesteps)
     tvec = time_row(timesteps, time_in, time_out, ready)
     ready("text")
-    emb_u = tvec + text_row(empty[...], text_proj)
-
-    pred_u = [[None] * frames for _ in range(rows)]
-    pred_c = [[None] * frames for _ in range(rows)]
-    steps_u = sample_steps(
-        emb_u, weight, first_in, wcat, wt, last, (state_u, xs_u, xt_u), consts, sizes, pred_u, ready
-    )
-    for _ in range(EARLY):
-        next(steps_u)
+    emb[0] = tvec
+    emb[1] = tvec + text_row(empty[...], text_proj)
 
     ready("table")
     partial[...] = jnp.sum(dot(counts, table[...]), axis=0, keepdims=True)
@@ -357,34 +333,35 @@
         pooled_copy(k).start()
     pool[me] = partial[...]
 
-    for _ in range(LEAD - EARLY):
-        next(steps_u)
-
     for s in range(sections):
         ready("spatial", s)
         ready("temporal", s)
-    for k in range(1, n):
-        slot = lax.rem(me + k, n)
-        pltpu.make_async_remote_copy(
-            src_ref=partial, dst_ref=pool.at[slot], send_sem=sendp.at[0], recv_sem=recvp.at[slot],
-            device_id=to(slot), device_id_type=mesh_id,
-        ).wait_recv()
-    pooled = pool[0]
-    for k in range(1, n):
-        pooled = pooled + pool[k]
-    emb_c = tvec + text_row(pooled * (1.0 / prompt.shape[0]), text_proj)
-    steps_c = sample_steps(
-        emb_c, weight, first_in, wcat, wt, last, (state_c, xs_c, xt_c), consts, sizes, pred_c, ready
-    )
-    live = True
-    while live:
-        live = next(steps_c, 0) is None
-        next(steps_u, 0)
-
+
+    def turn(i, carry):
+        @pl.when(i == 1)
+        def _():
+            for k in range(1, n):
+                slot = lax.rem(me + k, n)
+                pltpu.make_async_remote_copy(
+                    src_ref=partial, dst_ref=pool.at[slot], send_sem=sendp.at[0],
+                    recv_sem=recvp.at[slot], device_id=to(slot), device_id_type=mesh_id,
+                ).wait_recv()
+            pooled = pool[0]
+            for k in range(1, n):
+                pooled = pooled + pool[k]
+            emb[0] = emb[0] + text_row(pooled * (1.0 / prompt.shape[0]), text_proj)
+
+        sample(
+            emb[1 - i], weight_ref[...], first_in, wcat, wt, last, (state, xs, xt), consts, sizes,
+            predicted.at[i],
+        )
+        return carry
+
+    lax.fori_loop(0, 2, turn, 0)
     for r in range(rows):
         for f in range(frames):
-            without = pred_u[r][f]
-            guided = without + GUIDANCE_SCALE * (pred_c[r][f] - without)
+            without = predicted[0, r, f]
+            guided = without + GUIDANCE_SCALE * (predicted[1, r, f] - without)
             for l in range(lat):
                 drift[l * frames + f, pl.ds(r, 1), :] = (
                     keep * latent[0, l, f, pl.ds(r, 1), :]
@@ -501,7 +478,7 @@
     piece = (rows, cols)
     time_out, text_proj = time_out.T, text_proj.T
     conv_first = conv_first.transpose(0, 2, 1)
-    sample = [
+    sample_scratch = [
         pltpu.VMEM((rows * channels, width), BF16),
         pltpu.VMEM((rows * PAD, width), BF16),
         pltpu.VMEM((PAD, rows * width), BF16),
@@ -519,8 +496,11 @@
             pltpu.VMEM((sections, channels, PAD), BF16),
             pltpu.VMEM((56, width), F32),
         ]
-        + sample * 2
+        + sample_scratch
         + [
+            pltpu.VMEM((2, 1, channels), F32),
+            pltpu.VMEM((2, rows, frames, lat, cols), F32),
+            pltpu.VMEM((channels, 40), BF16),
             pltpu.VMEM((1, token_table.shape[1]), F32),
             pltpu.VMEM((n, 1, token_table.shape[1]), F32),
             pltpu.VMEM((pieces,) + piece, F32),

time: 40.3 us -> 41 us (1.017)
  Pallas kernels: 38.8 us -> 39.5 us
    pallas_call x1, Pallas kernels: 37.4 us -> 38.1 us  [local(): pl.pallas_call(functools.partial(sweep_kernel, n), out_shape=jax.ShapeDty...]
where the time goes in v4:
time: 41 us; the launch traced here: 40.8 us
  Pallas kernels  39.5 us (96%)
  between operations  1.29 us (3%)
    pallas_call x1, Pallas kernels, local(): pl.pallas_call(functools.partial(sweep_kernel, n), out_shape=jax.ShapeDty...  38.1 us
    pallas_call x1, Pallas kernels, local(): pl.pallas_call(split_kernel, out_shape=(shape, shape), in_specs=[VMEM], o...  1.38 us

profile of v4, /device:TPU:0, one launch (start us, length us, event | category | flops | bytes accessed | tf_op | source)
XLA Modules:
  0.0 40.8 jit_solution(9685343657074153134)
XLA Ops:
  1.3 38.1 %sweep.1.both = f32[16,2,2,128]{3,2,1,0:T(2,128)} custom-call(s32[77]{0:T(128)} %prompt.1, s32[1]{0:T(128)S(6)} %copy.16.timesteps, f32[1,1024]{1,0:T(1,128)} %bitcast.13, f32[16,2,128]{2,1,0:T(2,128)} %bitcast.10, f32[1,4,4,2,128]{4,3,2,1,0:T(2,128)} %latent.1, f32[1,4,4,2,128]{4,3,2,1,0:T(2,128)} %fresh.1, bf16[9,4,320]{2,1,0:T(4,128)(2,1)} %bitcast.9, ...), custom_call_target="tpu_custom_call" | custom-call | flops 8000000000 | bytes 14000000 | tf_op jit(solution)/shard_map/sweep/pallas_call | solution.py:487
  39.4 1.4 %split.1 = (f32[16,2,128]{2,1,0:T(2,128)}, f32[16,2,128]{2,1,0:T(2,128)}) custom-call(f32[16,2,2,128]{3,2,1,0:T(2,128)} %sweep.1.both), custom_call_target="tpu_custom_call" | custom-call | tf_op jit(solution)/shard_map/split/pallas_call | solution.py:529
